TPU v7x, 256 devices: a whole 4x4x8 slice. The times are simulated.
256 devices in a mesh: row: 8 (over z), col: 4 (over y), layer: 8 (over x, core).
Axes of the slice: x: 4, y: 4, z: 8, core: 2. Of those that a mesh axis runs over, the one named last changes fastest.
Arguments:
- fine_operator: bfloat16 [12288, 12288], P('row', ('layer', 'col')), may hold values from -0.0546875 to 0.0546875
- operator_pattern: int32 [192, 192], P('row', ('layer', 'col')), may hold values from 0 to 1
- prolongation: bfloat16 [12288, 4096], P(('layer', 'row'), 'col'), may hold values from -6 to 6
- prolong_pattern: int32 [192, 64], P(('layer', 'row'), 'col'), may hold values from 0 to 1
- restriction: bfloat16 [4096, 12288], P('col', ('row', 'layer')), may hold values from -0.15625 to 0.15625
- restrict_pattern: int32 [64, 192], P('col', ('row', 'layer')), may hold values from 0 to 1
Outputs:
- operator_prolong: bfloat16 [12288, 4096], P(('row', 'layer'), 'col')
- coarse_operator: float32 [4096, 4096], P(('row', 'layer'), 'col')
All inputs are finite; a program needn't handle non-finite values.
Results may differ from a plain program's by a relative error of at most 0.0029.
Values may be sent and summed in bfloat16 or wider, within the bound.
No kernel may reach another device: no remote copies, remote signals or barrier semaphores. Data moves between devices by JAX's collectives and lax.ppermute only.
A program may use at most 64 MiB of HBM per device.

v0:
```python
import jax
import jax.numpy as jnp
from jax import lax
from jax.sharding import PartitionSpec as P

BS = 64


def apply_pattern(values, pattern):
    height, breadth = values.shape
    blocks = values.reshape(height // BS, BS, breadth // BS, BS)
    factor = pattern.astype(values.dtype)[:, None, :, None]
    return (blocks * factor).reshape(height, breadth)


def on_device(
    fine_operator, operator_pattern, prolongation, prolong_pattern, restriction, restrict_pattern
):
    masked_operator = apply_pattern(fine_operator, operator_pattern)
    masked_prolong = apply_pattern(prolongation, prolong_pattern)
    masked_restrict = apply_pattern(restriction, restrict_pattern)
    inner_prolong = lax.all_gather(masked_prolong, "row", axis=0, tiled=True)
    partial_product = jnp.dot(
        lax.all_gather(masked_operator, "col", axis=1, tiled=True),
        inner_prolong,
        preferred_element_type=jnp.float32,
    )
    operator_prolong = lax.psum_scatter(
        partial_product, "layer", scatter_dimension=0, tiled=True
    ).astype(jnp.bfloat16)
    restrict_cols = lax.all_gather(masked_restrict, "col", axis=0, tiled=True)
    coarse_operator = lax.psum_scatter(
        jnp.dot(restrict_cols, operator_prolong, preferred_element_type=jnp.float32),
        ("row", "layer"),
        scatter_dimension=0,
        tiled=True,
    )
    return (operator_prolong, coarse_operator)


def solution(mesh):
    placed = (
        P("row", ("layer", "col")),
        P("row", ("layer", "col")),
        P(("layer", "row"), "col"),
        P(("layer", "row"), "col"),
        P("col", ("row", "layer")),
        P("col", ("row", "layer")),
    )
    return jax.shard_map(
        on_device,
        mesh=mesh,
        in_specs=placed,
        out_specs=(P(("row", "layer"), "col"), P(("row", "layer"), "col")),
        check_vma=False,
    )
```

profile of v0, /device:TPU:1, one launch (start us, length us, event | category | flops | bytes accessed | tf_op | source)
XLA Modules:
  0.0 402.9 jit_solution(16064793198763560805)
XLA Ops:
  7.2 0.0 all-gather.6.cloned.1.call-start
  7.2 0.8 convert_element_type.13
  8.0 0.2 mul.36
  8.2 0.5 mul.37
  8.7 1.9 mul.38
  10.6 0.0 all-gather.6.cloned.1.call-update
  10.6 0.0 all-gather.4.cloned.1.call-start
  10.7 1.5 copy.9
  12.2 0.4 mul.33
  12.6 1.5 mul.34
  14.1 2.6 mul.35
  16.7 0.0 all-gather.4.cloned.1.call-update
  16.7 0.0 reduce-scatter.3.cloned.1.call-start
  16.7 42.6 %all-gather.6.cloned.1.call-done = bf16[1536,1024]{1,0:T(8,128)(2,1)} async-done(((bf16[192,1024]{1,0:T(8,128)(2,1)}), bf16[1536,1024]{1,0:T(8,128)(2,1)}) %all-gather.6.cloned.1.call-update) | async-done | bytes 3145744 | tf_op jit(solution)/shard_map/all_gather | solution.py:22
  59.3 55.9 %all-gather.4.cloned.1.call-done = bf16[1536,1536]{0,1:T(8,128)(2,1)} async-done(((bf16[1536,384]{0,1:T(8,128)(2,1)}), bf16[1536,1536]{0,1:T(8,128)(2,1)}) %all-gather.4.cloned.1.call-update) | async-done | bytes 4718608 | tf_op jit(solution)/shard_map/all_gather | solution.py:24
  115.2 9.9 %fusion = f32[1536,1024]{1,0:T(8,128)} fusion(bf16[1536,1536]{0,1:T(8,128)(2,1)} %all-gather.4.cloned.1.call-done, bf16[1536,1024]{1,0:T(8,128)(2,1)} %all-gather.6.cloned.1.call-done), kind=kOutput, calls=%fused_computation | convolution fusion | flops 4831838208 | bytes 14155776 | tf_op jit(solution)/shard_map/dot_general | solution.py:23
  125.1 0.0 reduce-scatter.3.cloned.1.call-update
  125.1 0.0 all-gather.8.cloned.1.call-start
  125.2 0.6 copy-done.4
  125.8 0.2 mul.39
  126.0 0.5 mul.40
  126.5 0.0 copy-done.2
  126.5 0.9 mul.41
  127.4 0.0 all-gather.8.cloned.1.call-update
  127.4 0.0 reduce-scatter.5.cloned.1.call-start
  127.5 42.6 %reduce-scatter.3.cloned.1.call-done = f32[192,1024]{1,0:T(8,128)} async-done(((f32[1536,1024]{1,0:T(8,128)}), f32[192,1024]{1,0:T(8,128)}) %reduce-scatter.3.cloned.1.call-update) | async-done | bytes 786448 | tf_op jit(solution)/shard_map/reduce_scatter | solution.py:28
  170.1 1.2 convert_element_type.14
  171.3 0.0 copy-start
  171.3 29.9 %all-gather.8.cloned.1.call-done = bf16[4096,192]{0,1:T(8,128)(2,1)} async-done(((bf16[1024,192]{0,1:T(8,128)(2,1)}), bf16[4096,192]{0,1:T(8,128)(2,1)}) %all-gather.8.cloned.1.call-update) | async-done | bytes 1572880 | tf_op jit(solution)/shard_map/all_gather | solution.py:31
  201.3 9.5 %fusion.1 = f32[4096,1024]{1,0:T(8,128)} fusion(bf16[4096,192]{0,1:T(8,128)(2,1)} %all-gather.8.cloned.1.call-done, bf16[192,1024]{1,0:T(8,128)(2,1)S(1)} %convert_element_type.14), kind=kOutput, calls=%fused_computation.1 | convolution fusion | flops 1610612736 | bytes 18743296 | tf_op jit(solution)/shard_map/dot_general | solution.py:33
  210.8 0.0 reduce-scatter.5.cloned.1.call-update
  210.8 185.5 %reduce-scatter.5.cloned.1.call-done = f32[64,1024]{1,0:T(8,128)} async-done(((f32[4096,1024]{1,0:T(8,128)}), f32[64,1024]{1,0:T(8,128)}) %reduce-scatter.5.cloned.1.call-update) | async-done | bytes 262160 | tf_op jit(solution)/shard_map/reduce_scatter | solution.py:32
  (9 shorter events, 0.0 us)
Async XLA Ops:
  7.2 3.5 copy-start.3
  7.2 3.5 copy-start.1
  7.2 52.2 %all-gather.6.cloned.1.call-start = ((), (), s32[]{:S(2)}) async-start(), calls=%async_computation.3 | async-start | bytes 3538944 | tf_op jit(solution)/shard_map/all_gather | solution.py:22
  10.6 104.6 %all-gather.4.cloned.1.call-start = ((), (), s32[]{:S(2)}) async-start(), calls=%async_computation.2 | async-start | bytes 5898240 | tf_op jit(solution)/shard_map/all_gather | solution.py:24
  16.7 153.4 %reduce-scatter.3.cloned.1.call-start = ((), (), s32[]{:S(2)}) async-start(), calls=%async_computation.4 | async-start | bytes 7077888 | tf_op jit(solution)/shard_map/reduce_scatter | solution.py:28
  125.1 0.7 copy-start.4
  125.1 1.4 copy-start.2
  125.1 76.1 %all-gather.8.cloned.1.call-start = ((), (), s32[]{:S(2)}) async-start(), calls=%async_computation.5 | async-start | bytes 1966080 | tf_op jit(solution)/shard_map/all_gather | solution.py:31
  127.4 268.9 %reduce-scatter.5.cloned.1.call-start = ((), (), s32[]{:S(2)}) async-start(), calls=%async_computation.6 | async-start | bytes 17039360 | tf_op jit(solution)/shard_map/reduce_scatter | solution.py:32
  171.3 39.5 %copy-start = (bf16[192,1024]{1,0:T(8,128)(2,1)}, bf16[192,1024]{1,0:T(8,128)(2,1)S(1)}, u32[]{:S(2)}) copy-start(bf16[192,1024]{1,0:T(8,128)(2,1)S(1)} %convert_element_type.14) | copy-start | bytes 1179652
Sparse Core Ops, SparseCore 0:
  10.7 48.5 all-gather.5
  61.1 54.0 all-gather.3
  125.3 44.8 reduce-scatter.2
  171.8 29.4 all-gather.7
  210.9 185.3 reduce-scatter.4
where the time goes:
time: 406 us; the launch traced here: 403 us
  waiting for transfers between devices  357 us (88%)
  matrix products  19.4 us (5%)
  between operations  13.9 us (3%)
  other arithmetic  7.33 us (2%)
  local copies, waits for them, and re-layouts  5.4 us (1%)
    reduce_scatter x1, waiting for transfers between devices, on_device(): lax.psum_scatter(jnp.dot(restrict_cols, operator_prolong, preferred_eleme...  185 us
    all_gather x1, waiting for transfers between devices, on_device(): lax.all_gather(masked_operator, 'col', axis=1, tiled=True)  55.9 us
    reduce_scatter x1, waiting for transfers between devices, on_device(): lax.psum_scatter(partial_product, 'layer', scatter_dimension=0, tiled=True)  42.6 us
    all_gather x1, waiting for transfers between devices, on_device(): inner_prolong = lax.all_gather(masked_prolong, 'row', axis=0, tiled=True)  42.6 us
    all_gather x1, waiting for transfers between devices, on_device(): restrict_cols = lax.all_gather(masked_restrict, 'col', axis=0, tiled=True)  29.9 us
    dot_general x1, matrix products, on_device(): jnp.dot(lax.all_gather(masked_operator, 'col', axis=1, tiled=True), inner...  9.87 us
    dot_general x1, matrix products, on_device(): jnp.dot(restrict_cols, operator_prolong, preferred_element_type=jnp.float32)  9.54 us
  transfers between devices with their start and end apart: 5, of which 5 were waited for; matrix products, arithmetic and copies ran while one was open for 2% of the time, Pallas kernels for 0%

commit v1 on v0

v1 whole, which is shorter than its diff:
```python
import functools

import jax
import jax.numpy as jnp
from jax import lax
from jax.experimental import pallas as pl
from jax.experimental.pallas import tpu as pltpu
from jax.sharding import PartitionSpec as P

BS = 64
BF = jnp.bfloat16
F32 = jnp.float32
NCH = 2
SLOT_X = (2, 1, 3, 0)


def shift(v, axis, step):
    size = lax.axis_size(axis)
    step = step * 2 if axis == "layer" else step
    return lax.ppermute(v, axis, [(i, (i + step) % size) for i in range(size)])


def swap_cores(v):
    size = lax.axis_size("layer")
    return lax.ppermute(v, "layer", [(i, i ^ 1) for i in range(size)])


def dot(a, b):
    return jnp.dot(a, b, preferred_element_type=F32)


def lane_factor(pattern_ref, block_row, first, blocks):
    lane = lax.broadcasted_iota(jnp.int32, (1, blocks * BS), 1) // BS
    row = jnp.zeros((1, blocks * BS), F32)
    for j in range(blocks):
        row = jnp.where(lane == j, pattern_ref[first + j, block_row].astype(F32), row)
    return row.astype(BF)


def mask_operator_kernel(at_ref, pattern_ref, a_ref, o_ref):
    x, c = at_ref[0], at_ref[1]
    for half in range(2):
        core = (1 - c) if half == 0 else c
        for slot in range(4):
            source = (lax.rem(x + SLOT_X[slot], 4) * 2 + core) * 3
            for b in range(3):
                row = pl.multiple_of((source + b) * BS, BS)
                factor = lane_factor(pattern_ref, source + b, 0, 6)
                o_ref[pl.ds(((half * 4 + slot) * 3 + b) * BS, BS), :] = (
                    a_ref[pl.ds(row, BS), :] * factor
                )


def mask_prolong_kernel(pattern_ref, p_ref, o_ref):
    for b in range(3):
        lane = lax.broadcasted_iota(jnp.int32, (1, 1024), 1) // BS
        row = jnp.zeros((1, 1024), F32)
        for j in range(16):
            row = jnp.where(lane == j, pattern_ref[b, j].astype(F32), row)
        rows = slice(b * BS, (b + 1) * BS)
        o_ref[rows, :] = p_ref[rows, :] * row.astype(BF)


def mask_restrict_kernel(pattern_ref, r_ref, o_ref):
    lane = lax.broadcasted_iota(jnp.int32, (1, 128), 1) // BS
    for slot in range(4):
        to = slot
        for zz in range(2):
            block = zz * 8 + to * 2
            column = block * BS
            for b in range(3):
                low = pattern_ref[b, block].astype(F32)
                high = pattern_ref[b, block + 1].astype(F32)
                factor = jnp.where(lane == 0, low, high).astype(BF)
                rows = slice(b * BS, (b + 1) * BS)
                o_ref[slot, rows, zz * 128 : (zz + 1) * 128] = (
                    r_ref[rows, column : column + 128] * factor
                )


SMEM = pl.BlockSpec(memory_space=pltpu.SMEM)
VMEM = pl.BlockSpec(memory_space=pltpu.VMEM)


def local(kernel, shape, specs, name):
    return pl.pallas_call(
        kernel,
        out_shape=jax.ShapeDtypeStruct(shape, BF),
        in_specs=specs,
        out_specs=VMEM,
        name=name,
    )


def after(v, *others):
    return lax.optimization_barrier((v, others))[0]


def from_ring(v, axis):
    return shift(v, axis, 2), shift(v, axis, -1), shift(v, axis, 1), v


def on_device(
    fine_operator, operator_pattern, prolongation, prolong_pattern, restriction, restrict_pattern
):
    layer = lax.axis_index("layer")
    y = lax.axis_index("col")
    z = lax.axis_index("row")
    x, c = layer // 2, layer % 2
    at = jnp.stack([x, c]).astype(jnp.int32)

    a0 = local(mask_operator_kernel, (1536, 384), [SMEM, SMEM, VMEM], "mask_operator")(
        at, operator_pattern.T, fine_operator
    )
    p0 = local(mask_prolong_kernel, (192, 1024), [SMEM, VMEM], "mask_prolong")(
        *after((prolong_pattern, prolongation), a0)
    )
    r0 = local(mask_restrict_kernel, (4, 192, 256), [SMEM, VMEM], "mask_restrict")(
        restrict_pattern.T, restriction.T
    )

    a_left, a_right = shift(a0, "col", 1), shift(a0, "col", -1)

    p_full = jnp.zeros((8, 192, 1024), BF)

    def put(full, block, dz, first=0):
        return lax.dynamic_update_slice(full, block[None], (lax.rem(z + dz + 8, 8), first, 0))

    p_full = put(p_full, p0, 0)
    up, down = p0, p0
    for d in range(1, 4):
        up, down = shift(up, "row", 1), shift(down, "row", -1)
        p_full = put(put(p_full, up, -d), down, d)
        if d == 1:
            r0 = after(r0, up, down)
            size = lax.axis_size("layer")
            groups = [list(range(core, size, 2)) for core in range(2)]
            r_x = lax.all_to_all(r0, "layer", 0, 0, tiled=False, axis_index_groups=groups)
            r_x = jnp.concatenate(
                [
                    lax.dynamic_index_in_dim(r_x, lax.rem(x + slot, 4), 0, keepdims=False)
                    for slot in SLOT_X
                ],
                0,
            )
        if d == 2:
            up, down = after((up, down), r_x)
    p_full = put(p_full, shift(up[:96], "row", 1), -4)
    p_full = put(p_full, shift(down[96:], "row", -1), 4, 96)
    p_full = p_full.reshape(4, 384, 1024)

    def p_of(dy):
        return lax.dynamic_index_in_dim(p_full, lax.rem(y + dy + 4, 4), 0, keepdims=False)

    a_top = shift(a_left[:768], "col", 1)
    a_bottom = shift(a_right[768:], "col", -1)
    a_top = after(a_top, a_bottom)

    r_far, r_right, r_left, r_x = from_ring(after(r_x, a_top, a_bottom), "col")

    acc = dot(a0, p_of(0)) + dot(a_left, p_of(-1)) + dot(a_right, p_of(1))
    p_far = p_of(2)
    width = 1024 // NCH
    outs, coarse = [], []
    for n in range(NCH):
        cols = slice(n * width, (n + 1) * width)
        away = acc[:768, cols] + dot(a_top, p_far[:, cols])
        mine = acc[768:, cols] + dot(a_bottom, p_far[:, cols])
        s = mine + swap_cores(away)
        far, ahead, behind, own = s[:192], s[192:384], s[384:576], s[576:]
        far_top = shift(far[:96], "layer", 1)
        far_bottom = shift(far[96:], "layer", -1)
        ahead = ahead + jnp.pad(far_top, ((0, 96), (0, 0)))
        behind = behind + jnp.pad(far_bottom, ((96, 0), (0, 0)))
        block = (own + shift(ahead, "layer", 1) + shift(behind, "layer", -1)).astype(BF)
        outs.append(block)
        if n == 0:
            r_blocks = after((r_far, r_right, r_left, r_x), block)
            r_full = jnp.zeros((4, 768, 256), BF)
            for piece, dy in zip(r_blocks, (2, 1, 3, 0)):
                r_full = lax.dynamic_update_slice(
                    r_full, piece[None], (lax.rem(y + dy, 4), 0, 0)
                )
            r_full = r_full.transpose(0, 2, 1).reshape(8, 128, 768)
            r_full = lax.dynamic_slice_in_dim(jnp.concatenate([r_full, r_full], 0), z, 8, 0)
            r_full = r_full.reshape(8, 2, 64, 768)
            r_away = lax.dynamic_index_in_dim(r_full, 1 - c, 1, keepdims=False).reshape(512, 768)
            r_mine = lax.dynamic_index_in_dim(r_full, c, 1, keepdims=False).reshape(512, 768)
        b = jnp.concatenate(from_ring(block, "layer"), 0)
        q = dot(r_mine, b) + swap_cores(dot(r_away, b))
        coarse.append(q.reshape(8, 64, width))
    q = jnp.concatenate(coarse, 2)
    q0 = q[0]
    q = lax.dynamic_slice_in_dim(jnp.concatenate([q, q], 0).astype(BF), lax.rem(8 - z, 8), 8, 0)
    q = lax.all_to_all(q, "row", 0, 0, tiled=False)
    q = jnp.where(lax.broadcasted_iota(jnp.int32, q.shape, 0) == z, 0.0, q.astype(F32))
    return jnp.concatenate(outs, 1), q0 + jnp.sum(q, 0)


def solution(mesh):
    placed = (
        P("row", ("layer", "col")),
        P("row", ("layer", "col")),
        P(("layer", "row"), "col"),
        P(("layer", "row"), "col"),
        P("col", ("row", "layer")),
        P("col", ("row", "layer")),
    )
    return jax.shard_map(
        on_device,
        mesh=mesh,
        in_specs=placed,
        out_specs=(P(("row", "layer"), "col"), P(("row", "layer"), "col")),
        check_vma=False,
    )
```

time: 406 us -> 170 us (0.42)
  waiting for transfers between devices: 357 us -> 61.5 us
  starting transfers between devices: 0.21 us -> 59.2 us
  between operations: 13.9 us -> 1.06 us
  Pallas kernels: 0 us -> 6.2 us
  local copies, waits for them, and re-layouts: 5.4 us -> 11.5 us
    reduce_scatter x2 -> x0, waiting for transfers between devices: 228 us -> none  [the longest x1 185 us: on_device(): lax.psum_scatter(jnp.dot(restrict_cols, operator_prolong, preferred_eleme...]
    all_gather x3 -> x0, waiting for transfers between devices: 128 us -> none  [the longest x1 55.9 us: on_device(): lax.all_gather(masked_operator, 'col', axis=1, tiled=True)]
    ppermute x0 -> x33, starting transfers between devices: none -> 50.9 us  [the longest x29 38.7 us: shift(): return lax.ppermute(v, axis, [(i, (i + step) % size) for i in range(size)])]
    ppermute x0 -> x33, waiting for transfers between devices: none -> 32.6 us  [the longest x29 29.3 us: shift(): return lax.ppermute(v, axis, [(i, (i + step) % size) for i in range(size)])]
    all_to_all x0 -> x2, waiting for transfers between devices: none -> 29 us  [the longest x1 27.4 us: on_device(): q = lax.all_to_all(q, 'row', 0, 0, tiled=False)]
    all_to_all x0 -> x2, starting transfers between devices: none -> 8.35 us  [the longest x1 4.34 us: on_device(): q = lax.all_to_all(q, 'row', 0, 0, tiled=False)]
    pallas_call x0 -> x3, Pallas kernels: none -> 6.2 us  [the longest x1 2.55 us: on_device(): local(mask_operator_kernel, (1536, 384), [SMEM, SMEM, VMEM], 'mask_operat...]
    mul x3 -> x0, other arithmetic: 5.36 us -> none  [apply_pattern(): return (blocks * factor).reshape(height, breadth)]
  transfers between devices with their start and end apart: 5 -> 35, of which waited for: 5 -> 15; matrix products, arithmetic and copies ran while one was open for 2% -> 20% of each run, Pallas kernels for 0% -> 1%
where the time goes in v1:
time: 170 us; the launch traced here: 169 us
  waiting for transfers between devices  61.5 us (36%)
  starting transfers between devices  59.2 us (35%)
  matrix products  18.4 us (11%)
  local copies, waits for them, and re-layouts  11.5 us (7%)
  other arithmetic  11.3 us (7%)
  Pallas kernels  6.2 us (4%)
    ppermute x29, starting transfers between devices, shift(): return lax.ppermute(v, axis, [(i, (i + step) % size) for i in range(size)])  38.7 us
    ppermute x29, waiting for transfers between devices, shift(): return lax.ppermute(v, axis, [(i, (i + step) % size) for i in range(size)])  29.3 us
    all_to_all x1, waiting for transfers between devices, on_device(): q = lax.all_to_all(q, 'row', 0, 0, tiled=False)  27.4 us
    dot_general x11, matrix products, dot(): return jnp.dot(a, b, preferred_element_type=F32)  18.4 us
    ppermute x4, starting transfers between devices, swap_cores(): return lax.ppermute(v, 'layer', [(i, i ^ 1) for i in range(size)])  12.2 us
    all_to_all x1, starting transfers between devices, on_device(): q = lax.all_to_all(q, 'row', 0, 0, tiled=False)  4.34 us
    dynamic_update_slice x9, local copies, waits for them, and re-layouts, put(): lax.dynamic_update_slice(full, block[None], (lax.rem(z + dz + 8, 8), firs...  4.25 us
    all_to_all x1, starting transfers between devices, on_device(): lax.all_to_all(r0, 'layer', 0, 0, tiled=False, axis_index_groups=groups)  4.01 us
  transfers between devices with their start and end apart: 35, of which 15 were waited for; matrix products, arithmetic and copies ran while one was open for 20% of the time, Pallas kernels for 1%

profile of v1, /device:TPU:1, one launch (start us, length us, event | category | flops | bytes accessed | tf_op | source)
XLA Modules:
  0.0 169.1 jit_solution(17828613941708374815)
XLA Ops:
  1.2 2.5 %mask_operator.1 = bf16[1536,384]{1,0:T(8,128)(2,1)} custom-call(s32[2]{0:T(128)} %pad_add_fusion.at_ref, s32[6,24]{1,0:T(8,128)} %bitcast.87, bf16[1536,384]{1,0:T(8,128)(2,1)} %a_ref.1), custom_call_target="tpu_custom_call" | custom-call | tf_op jit(solution)/shard_map/mask_operator/pallas_call | solution.py:112
  5.6 2.5 %collective-permute-start = (bf16[192,1024]{1,0:T(8,128)(2,1)}, bf16[192,1024]{1,0:T(8,128)(2,1)}, u32[]{:S(2)}, u32[]{:S(2)}) collective-permute-start(bf16[192,1024]{1,0:T(8,128)(2,1)} %mask_prolong.1), channel_id=1, source_target_pairs={{0,32},{32,64},{64,96},{96,128},{128,160},{160,192},{192,224},{224... | collective-permute-start | bytes 1179656 | tf_op jit(solution)/shard_map/ppermute | solution.py:20
  8.1 3.9 %collective-permute-start.1 = (bf16[192,1024]{1,0:T(8,128)(2,1)}, bf16[192,1024]{1,0:T(8,128)(2,1)S(1)}, u32[]{:S(2)}, u32[]{:S(2)}) collective-permute-start(bf16[192,1024]{1,0:T(8,128)(2,1)} %mask_prolong.1), channel_id=1, source_target_pairs={{0,224},{32,0},{64,32},{96,64},{128,96},{160,128},{192,160},{224,1... | collective-permute-start | bytes 1179656 | tf_op jit(solution)/shard_map/ppermute | solution.py:20
  14.7 1.9 %mask_restrict.1 = bf16[4,192,256]{2,1,0:T(8,128)(2,1)} custom-call(s32[3,16]{1,0:T(4,128)} %bitcast.88, bf16[192,1024]{1,0:T(8,128)(2,1)} %bitcast.85), custom_call_target="tpu_custom_call" | custom-call | tf_op jit(solution)/shard_map/mask_restrict/pallas_call | solution.py:118
  17.6 3.5 %collective-permute-done = bf16[192,1024]{1,0:T(8,128)(2,1)} collective-permute-done((bf16[192,1024]{1,0:T(8,128)(2,1)}, bf16[192,1024]{1,0:T(8,128)(2,1)}, u32[]{:S(2)}, u32[]{:S(2)}) %collective-permute-start) | collective-permute-done | bytes 393248 | tf_op jit(solution)/shard_map/ppermute | solution.py:20
  21.9 4.0 %all-to-all-start = ((bf16[4,192,256]{2,1,0:T(8,128)(2,1)}), bf16[4,192,256]{2,1,0:T(8,128)(2,1)S(1)}, u32[]{:S(2)}, u32[]{:S(2)}) async-start(bf16[4,192,256]{2,1,0:T(8,128)(2,1)} %mask_restrict.1), calls=%async_computation | async-start | bytes 786432 | tf_op jit(solution)/shard_map/all_to_all | solution.py:138
  25.9 2.7 %collective-permute-start.3 = (bf16[192,1024]{1,0:T(8,128)(2,1)}, bf16[192,1024]{1,0:T(8,128)(2,1)}, u32[]{:S(2)}, u32[]{:S(2)}) collective-permute-start(bf16[192,1024]{1,0:T(8,128)(2,1)} %copy-done.4), channel_id=1, source_target_pairs={{0,224},{32,0},{64,32},{96,64},{128,96},{160,128},{192,160},{224,1... | collective-permute-start | bytes 1179656 | tf_op jit(solution)/shard_map/ppermute | solution.py:20
  32.3 4.3 %collective-permute-done.2 = bf16[192,1024]{1,0:T(8,128)(2,1)} collective-permute-done((bf16[192,1024]{1,0:T(8,128)(2,1)}, bf16[192,1024]{1,0:T(8,128)(2,1)}, u32[]{:S(2)}, u32[]{:S(2)}) %collective-permute-start.2) | collective-permute-done | bytes 393248 | tf_op jit(solution)/shard_map/ppermute | solution.py:20
  41.3 4.9 %collective-permute-done.4 = bf16[192,1024]{1,0:T(8,128)(2,1)S(1)} collective-permute-done((bf16[192,1024]{1,0:T(8,128)(2,1)}, bf16[192,1024]{1,0:T(8,128)(2,1)S(1)}, u32[]{:S(2)}, u32[]{:S(2)}) %collective-permute-start.4) | collective-permute-done | bytes 393248 | tf_op jit(solution)/shard_map/ppermute | solution.py:20
  46.3 2.7 %collective-permute-start.7 = (bf16[96,1024]{1,0:T(8,128)(2,1)S(1)}, bf16[96,1024]{1,0:T(8,128)(2,1)S(1)}, u32[]{:S(2)}, u32[]{:S(2)}) collective-permute-start(bf16[96,1024]{1,0:T(8,128)(2,1)S(1)} %slice.93), channel_id=1, source_target_pairs={{0,224},{32,0},{64,32},{96,64},{128,96},{160,128},{192,160},{224,1... | collective-permute-start | bytes 589832 | tf_op jit(solution)/shard_map/ppermute | solution.py:20
  50.1 2.8 %collective-permute-start.10 = (bf16[768,384]{1,0:T(8,128)(2,1)S(1)}, bf16[768,384]{1,0:T(8,128)(2,1)S(1)}, u32[]{:S(2)}, u32[]{:S(2)}) collective-permute-start(bf16[768,384]{1,0:T(8,128)(2,1)S(1)} %slice.95), channel_id=1, source_target_pairs={{0,24},{8,0},{16,8},{24,16},{1,25},{9,1},{17,9},{25,17},{2,26},{10... | collective-permute-start | bytes 1769480 | tf_op jit(solution)/shard_map/ppermute | solution.py:20
  54.5 1.8 %fusion.8 = f32[1536,1024]{1,0:T(8,128)S(1)} fusion(bf16[1536,384]{1,0:T(8,128)(2,1)S(1)} %copy-done, bf16[4,384,1024]{2,1,0:T(8,128)(2,1)S(1)} %bitcast.70, s32[]{:T(128)S(6)} %select_n.106), kind=kOutput, calls=%fused_computation.25 | convolution fusion | flops 1207959552 | bytes 8257540 | tf_op jit(solution)/shard_map/dot_general | solution.py:29
  56.4 3.1 %fusion.6 = f32[1536,1024]{1,0:T(8,128)S(1)} fusion(bf16[1536,384]{1,0:T(8,128)(2,1)} %collective-permute-done.8, bf16[4,384,1024]{2,1,0:T(8,128)(2,1)S(1)} %bitcast.72, s32[]{:T(128)S(6)} %select_n.107), kind=kOutput, calls=%fused_computation.23 | convolution fusion | flops 1207959552 | bytes 8257540 | tf_op jit(solution)/shard_map/dot_general | solution.py:29
  59.5 3.2 %add_add_fusion = f32[1536,1024]{1,0:T(8,128)S(1)} fusion(f32[1536,1024]{1,0:T(8,128)S(1)} %fusion.8, f32[1536,1024]{1,0:T(8,128)S(1)} %fusion.6, bf16[1536,384]{1,0:T(8,128)(2,1)} %collective-permute-done.9, bf16[4,384,1024]{2,1,0:T(8,128)(2,1)S(1)} %bitcast.73, s32[]{:T(128)S(6)} %select_n.108), kind=kOutput, calls=%fused_computation | convolution fusion | flops 1211105280 | bytes 20840452 | tf_op jit(solution)/shard_map/dot_general | solution.py:29
  62.7 3.5 %collective-permute-done.11 = bf16[768,384]{1,0:T(8,128)(2,1)S(1)} collective-permute-done((bf16[768,384]{1,0:T(8,128)(2,1)S(1)}, bf16[768,384]{1,0:T(8,128)(2,1)S(1)}, u32[]{:S(2)}, u32[]{:S(2)}) %collective-permute-start.11) | collective-permute-done | bytes 589856 | tf_op jit(solution)/shard_map/ppermute | solution.py:20
  66.8 5.2 %collective-permute-start.12 = (f32[768,512]{1,0:T(8,128)S(1)}, f32[768,512]{1,0:T(8,128)S(1)}, u32[]{:S(2)}, u32[]{:S(2)}) collective-permute-start(f32[768,512]{1,0:T(8,128)S(1)} %slice_add_fusion.2), channel_id=1, source_target_pairs={{0,1},{1,0},{2,3},{3,2},{4,5},{5,4},{6,7},{7,6},{8,9},{9,8},{10,11... | collective-permute-start | bytes 4718600 | tf_op jit(solution)/shard_map/ppermute | solution.py:25
  72.7 2.4 %collective-permute-done.12 = f32[768,512]{1,0:T(8,128)S(1)} collective-permute-done((f32[768,512]{1,0:T(8,128)S(1)}, f32[768,512]{1,0:T(8,128)S(1)}, u32[]{:S(2)}, u32[]{:S(2)}) %collective-permute-start.12) | collective-permute-done | bytes 1572896 | tf_op jit(solution)/shard_map/ppermute | solution.py:25
  79.2 2.7 %collective-permute-start.20 = (f32[96,512]{1,0:T(8,128)S(1)}, f32[96,512]{1,0:T(8,128)S(1)}, u32[]{:S(2)}, u32[]{:S(2)}) collective-permute-start(f32[96,512]{1,0:T(8,128)S(1)} %get-tuple-element.33), channel_id=1, source_target_pairs={{0,6},{1,7},{2,0},{3,1},{4,2},{5,3},{6,4},{7,5},{8,14},{9,15},{10,... | collective-permute-start | bytes 589832 | tf_op jit(solution)/shard_map/ppermute | solution.py:20
  84.6 2.1 %collective-permute-start.16 = (f32[192,512]{1,0:T(8,128)}, f32[192,512]{1,0:T(8,128)}, u32[]{:S(2)}, u32[]{:S(2)}) collective-permute-start(f32[192,512]{1,0:T(8,128)} %get-tuple-element.27), channel_id=1, source_target_pairs={{0,6},{1,7},{2,0},{3,1},{4,2},{5,3},{6,4},{7,5},{8,14},{9,15},{10,... | collective-permute-start | bytes 1179656 | tf_op jit(solution)/shard_map/ppermute | solution.py:20
  88.8 2.2 %collective-permute-start.21 = (f32[192,512]{1,0:T(8,128)}, f32[192,512]{1,0:T(8,128)}, u32[]{:S(2)}, u32[]{:S(2)}) collective-permute-start(f32[192,512]{1,0:T(8,128)} %get-tuple-element.31), channel_id=1, source_target_pairs={{0,6},{1,7},{2,0},{3,1},{4,2},{5,3},{6,4},{7,5},{8,14},{9,15},{10,... | collective-permute-start | bytes 1179656 | tf_op jit(solution)/shard_map/ppermute | solution.py:20
  91.0 3.2 %collective-permute-done.14 = f32[192,512]{1,0:T(8,128)} collective-permute-done((f32[192,512]{1,0:T(8,128)}, f32[192,512]{1,0:T(8,128)}, u32[]{:S(2)}, u32[]{:S(2)}) %collective-permute-start.14) | collective-permute-done | bytes 393248 | tf_op jit(solution)/shard_map/ppermute | solution.py:20
  95.7 1.9 %fusion.16 = bf16[192,512]{1,0:T(8,128)(2,1)} fusion(f32[192,512]{1,0:T(8,128)} %collective-permute-done.16, f32[192,512]{1,0:T(8,128)} %collective-permute-done.14, f32[768,512]{1,0:T(8,128)S(1)} %fusion.3), kind=kLoop, calls=%fused_computation.40 | loop fusion | flops 294912 | bytes 1376256 | tf_op jit(solution)/shard_map/convert_element_type | solution.py:175
  97.5 5.1 %collective-permute-done.19 = f32[192,512]{1,0:T(8,128)} collective-permute-done((f32[192,512]{1,0:T(8,128)}, f32[192,512]{1,0:T(8,128)}, u32[]{:S(2)}, u32[]{:S(2)}) %collective-permute-start.19) | collective-permute-done | bytes 393248 | tf_op jit(solution)/shard_map/ppermute | solution.py:20
  105.0 1.9 %fusion.14 = bf16[192,512]{1,0:T(8,128)(2,1)} fusion(f32[192,512]{1,0:T(8,128)} %collective-permute-done.21, f32[192,512]{1,0:T(8,128)} %collective-permute-done.19, f32[768,512]{1,0:T(8,128)S(1)} %fusion.2), kind=kLoop, calls=%fused_computation.35 | loop fusion | flops 294912 | bytes 1376256 | tf_op jit(solution)/shard_map/convert_element_type | solution.py:175
  106.9 2.0 %collective-permute-start.29 = (bf16[192,512]{1,0:T(8,128)(2,1)}, bf16[192,512]{1,0:T(8,128)(2,1)S(1)}, u32[]{:S(2)}, u32[]{:S(2)}) collective-permute-start(bf16[192,512]{1,0:T(8,128)(2,1)} %fusion.14), channel_id=1, source_target_pairs={{0,4},{1,5},{2,6},{3,7},{4,0},{5,1},{6,2},{7,3},{8,12},{9,13},{10,... | collective-permute-start | bytes 589832 | tf_op jit(solution)/shard_map/ppermute | solution.py:20
  117.3 4.7 %collective-permute-start.28 = (f32[512,512]{1,0:T(8,128)S(1)}, f32[512,512]{1,0:T(8,128)S(1)}, u32[]{:S(2)}, u32[]{:S(2)}) collective-permute-start(f32[512,512]{1,0:T(8,128)S(1)} %fusion.37), channel_id=1, source_target_pairs={{0,1},{1,0},{2,3},{3,2},{4,5},{5,4},{6,7},{7,6},{8,9},{9,8},{10,11... | collective-permute-start | bytes 3145736 | tf_op jit(solution)/shard_map/ppermute | solution.py:25
  123.7 2.6 %fusion.36 = f32[512,512]{1,0:T(8,128)} fusion(bf16[512,768]{1,0:T(8,128)(2,1)S(1)} %bitcast.84, bf16[192,512]{1,0:T(8,128)(2,1)} %fusion.14, bf16[192,512]{1,0:T(8,128)(2,1)S(1)} %collective-permute-done.31, bf16[192,512]{1,0:T(8,128)(2,1)S(1)} %collective-permute-done.30, bf16[192,512]{1,0:T(8,128)(2,1)S(1)} %collective-permute-done.29), kind=kOutput, calls=%fused_computation.63 | convolution fusion | flops 405798912 | bytes 2621440 | tf_op jit(solution)/shard_map/dot_general | solution.py:29
  126.3 2.2 %collective-permute-start.32 = (f32[512,512]{1,0:T(8,128)}, f32[512,512]{1,0:T(8,128)}, u32[]{:S(2)}, u32[]{:S(2)}) collective-permute-start(f32[512,512]{1,0:T(8,128)} %fusion.36), channel_id=1, source_target_pairs={{0,1},{1,0},{2,3},{3,2},{4,5},{5,4},{6,7},{7,6},{8,9},{9,8},{10,11... | collective-permute-start | bytes 3145736 | tf_op jit(solution)/shard_map/ppermute | solution.py:25
  131.1 1.9 %convolution_add_fusion = f32[512,512]{1,0:T(8,128)S(1)} fusion(f32[512,512]{1,0:T(8,128)} %collective-permute-done.32, bf16[512,768]{1,0:T(8,128)(2,1)S(1)} %bitcast.82, bf16[192,512]{1,0:T(8,128)(2,1)} %fusion.14, bf16[192,512]{1,0:T(8,128)(2,1)S(1)} %copy-done.6, bf16[192,512]{1,0:T(8,128)(2,1)S(1)} %collective-permute-done.30, ...), kind=kOutput, calls=%fused_computation.17 | convolution fusion | flops 406061056 | bytes 3670016 | tf_op jit(solution)/shard_map/dot_general | solution.py:29
  134.6 4.3 %all-to-all-start.1 = ((bf16[8,64,1024]{2,1,0:T(8,128)(2,1)}), bf16[8,64,1024]{2,1,0:T(8,128)(2,1)S(1)}, u32[]{:S(2)}, u32[]{:S(2)}) async-start(bf16[8,64,1024]{2,1,0:T(8,128)(2,1)} %fusion.4), calls=%async_computation.1 | async-start | bytes 2097152 | tf_op jit(solution)/shard_map/all_to_all | solution.py:195
  138.9 1.8 %pad_maximum_fusion.4 = bf16[192,1024]{1,0:T(8,128)(2,1)} fusion(bf16[192,512]{1,0:T(8,128)(2,1)} %fusion.14, bf16[192,512]{1,0:T(8,128)(2,1)} %fusion.16), kind=kLoop, calls=%fused_computation.42 | loop fusion | flops 786432 | bytes 786432 | tf_op jit(solution)/shard_map/concatenate | solution.py:197
  140.7 27.4 %all-to-all-done.1 = bf16[8,64,1024]{2,1,0:T(8,128)(2,1)S(1)} async-done(((bf16[8,64,1024]{2,1,0:T(8,128)(2,1)}), bf16[8,64,1024]{2,1,0:T(8,128)(2,1)S(1)}, u32[]{:S(2)}, u32[]{:S(2)}) %all-to-all-start.1) | async-done | bytes 1048608 | tf_op jit(solution)/shard_map/all_to_all | solution.py:195
  (107 shorter events, 47.4 us)
Async XLA Ops:
  5.6 15.6 %collective-permute-start = (bf16[192,1024]{1,0:T(8,128)(2,1)}, bf16[192,1024]{1,0:T(8,128)(2,1)}, u32[]{:S(2)}, u32[]{:S(2)}) collective-permute-start(bf16[192,1024]{1,0:T(8,128)(2,1)} %mask_prolong.1), channel_id=1, source_target_pairs={{0,32},{32,64},{64,96},{96,128},{128,160},{160,192},{192,224},{224... | collective-permute-start | bytes 1179656 | tf_op jit(solution)/shard_map/ppermute | solution.py:20
  8.1 13.1 %collective-permute-start.1 = (bf16[192,1024]{1,0:T(8,128)(2,1)}, bf16[192,1024]{1,0:T(8,128)(2,1)S(1)}, u32[]{:S(2)}, u32[]{:S(2)}) collective-permute-start(bf16[192,1024]{1,0:T(8,128)(2,1)} %mask_prolong.1), channel_id=1, source_target_pairs={{0,224},{32,0},{64,32},{96,64},{128,96},{160,128},{192,160},{224,1... | collective-permute-start | bytes 1179656 | tf_op jit(solution)/shard_map/ppermute | solution.py:20
  12.0 41.0 %collective-permute-start.8 = (bf16[1536,384]{1,0:T(8,128)(2,1)}, bf16[1536,384]{1,0:T(8,128)(2,1)}, u32[]{:S(2)}, u32[]{:S(2)}) collective-permute-start(bf16[1536,384]{1,0:T(8,128)(2,1)} %mask_operator.1), channel_id=1, source_target_pairs={{0,8},{8,16},{16,24},{24,0},{1,9},{9,17},{17,25},{25,1},{2,10},{10... | collective-permute-start | bytes 3538952 | tf_op jit(solution)/shard_map/ppermute | solution.py:20
  13.3 35.7 %collective-permute-start.9 = (bf16[1536,384]{1,0:T(8,128)(2,1)}, bf16[1536,384]{1,0:T(8,128)(2,1)}, u32[]{:S(2)}, u32[]{:S(2)}) collective-permute-start(bf16[1536,384]{1,0:T(8,128)(2,1)} %mask_operator.1), channel_id=1, source_target_pairs={{0,24},{8,0},{16,8},{24,16},{1,25},{9,1},{17,9},{25,17},{2,26},{10... | collective-permute-start | bytes 3538952 | tf_op jit(solution)/shard_map/ppermute | solution.py:20
  21.9 10.3 %all-to-all-start = ((bf16[4,192,256]{2,1,0:T(8,128)(2,1)}), bf16[4,192,256]{2,1,0:T(8,128)(2,1)S(1)}, u32[]{:S(2)}, u32[]{:S(2)}) async-start(bf16[4,192,256]{2,1,0:T(8,128)(2,1)} %mask_restrict.1), calls=%async_computation | async-start | bytes 786432 | tf_op jit(solution)/shard_map/all_to_all | solution.py:138
  25.9 10.6 %collective-permute-start.2 = (bf16[192,1024]{1,0:T(8,128)(2,1)}, bf16[192,1024]{1,0:T(8,128)(2,1)}, u32[]{:S(2)}, u32[]{:S(2)}) collective-permute-start(bf16[192,1024]{1,0:T(8,128)(2,1)} %collective-permute-done), channel_id=1, source_target_pairs={{0,32},{32,64},{64,96},{96,128},{128,160},{160,192},{192,224},{224... | collective-permute-start | bytes 1179656 | tf_op jit(solution)/shard_map/ppermute | solution.py:20
  25.9 10.6 %collective-permute-start.3 = (bf16[192,1024]{1,0:T(8,128)(2,1)}, bf16[192,1024]{1,0:T(8,128)(2,1)}, u32[]{:S(2)}, u32[]{:S(2)}) collective-permute-start(bf16[192,1024]{1,0:T(8,128)(2,1)} %copy-done.4), channel_id=1, source_target_pairs={{0,224},{32,0},{64,32},{96,64},{128,96},{160,128},{192,160},{224,1... | collective-permute-start | bytes 1179656 | tf_op jit(solution)/shard_map/ppermute | solution.py:20
  36.5 9.6 %collective-permute-start.4 = (bf16[192,1024]{1,0:T(8,128)(2,1)}, bf16[192,1024]{1,0:T(8,128)(2,1)S(1)}, u32[]{:S(2)}, u32[]{:S(2)}) collective-permute-start(bf16[192,1024]{1,0:T(8,128)(2,1)} %collective-permute-done.2), channel_id=1, source_target_pairs={{0,32},{32,64},{64,96},{96,128},{128,160},{160,192},{192,224},{224... | collective-permute-start | bytes 1179656 | tf_op jit(solution)/shard_map/ppermute | solution.py:20
  37.5 8.7 %collective-permute-start.5 = (bf16[192,1024]{1,0:T(8,128)(2,1)}, bf16[192,1024]{1,0:T(8,128)(2,1)S(1)}, u32[]{:S(2)}, u32[]{:S(2)}) collective-permute-start(bf16[192,1024]{1,0:T(8,128)(2,1)} %collective-permute-done.3), channel_id=1, source_target_pairs={{0,224},{32,0},{64,32},{96,64},{128,96},{160,128},{192,160},{224,1... | collective-permute-start | bytes 1179656 | tf_op jit(solution)/shard_map/ppermute | solution.py:20
  46.2 8.3 %collective-permute-start.6 = (bf16[96,1024]{1,0:T(8,128)(2,1)S(1)}, bf16[96,1024]{1,0:T(8,128)(2,1)S(1)}, u32[]{:S(2)}, u32[]{:S(2)}) collective-permute-start(bf16[96,1024]{1,0:T(8,128)(2,1)S(1)} %slice.92), channel_id=1, source_target_pairs={{0,32},{32,64},{64,96},{96,128},{128,160},{160,192},{192,224},{224... | collective-permute-start | bytes 589832 | tf_op jit(solution)/shard_map/ppermute | solution.py:20
  46.3 8.2 %collective-permute-start.7 = (bf16[96,1024]{1,0:T(8,128)(2,1)S(1)}, bf16[96,1024]{1,0:T(8,128)(2,1)S(1)}, u32[]{:S(2)}, u32[]{:S(2)}) collective-permute-start(bf16[96,1024]{1,0:T(8,128)(2,1)S(1)} %slice.93), channel_id=1, source_target_pairs={{0,224},{32,0},{64,32},{96,64},{128,96},{160,128},{192,160},{224,1... | collective-permute-start | bytes 589832 | tf_op jit(solution)/shard_map/ppermute | solution.py:20
  50.1 12.6 %collective-permute-start.10 = (bf16[768,384]{1,0:T(8,128)(2,1)S(1)}, bf16[768,384]{1,0:T(8,128)(2,1)S(1)}, u32[]{:S(2)}, u32[]{:S(2)}) collective-permute-start(bf16[768,384]{1,0:T(8,128)(2,1)S(1)} %slice.95), channel_id=1, source_target_pairs={{0,24},{8,0},{16,8},{24,16},{1,25},{9,1},{17,9},{25,17},{2,26},{10... | collective-permute-start | bytes 1769480 | tf_op jit(solution)/shard_map/ppermute | solution.py:20
  54.1 12.1 %collective-permute-start.11 = (bf16[768,384]{1,0:T(8,128)(2,1)S(1)}, bf16[768,384]{1,0:T(8,128)(2,1)S(1)}, u32[]{:S(2)}, u32[]{:S(2)}) collective-permute-start(bf16[768,384]{1,0:T(8,128)(2,1)S(1)} %slice.98), channel_id=1, source_target_pairs={{0,8},{8,16},{16,24},{24,0},{1,9},{9,17},{17,25},{25,1},{2,10},{10... | collective-permute-start | bytes 1769480 | tf_op jit(solution)/shard_map/ppermute | solution.py:20
  66.8 8.2 %collective-permute-start.12 = (f32[768,512]{1,0:T(8,128)S(1)}, f32[768,512]{1,0:T(8,128)S(1)}, u32[]{:S(2)}, u32[]{:S(2)}) collective-permute-start(f32[768,512]{1,0:T(8,128)S(1)} %slice_add_fusion.2), channel_id=1, source_target_pairs={{0,1},{1,0},{2,3},{3,2},{4,5},{5,4},{6,7},{7,6},{8,9},{9,8},{10,11... | collective-permute-start | bytes 4718600 | tf_op jit(solution)/shard_map/ppermute | solution.py:25
  75.7 7.4 %collective-permute-start.13 = (f32[96,512]{1,0:T(8,128)S(1)}, f32[96,512]{1,0:T(8,128)S(1)}, u32[]{:S(2)}, u32[]{:S(2)}) collective-permute-start(f32[96,512]{1,0:T(8,128)S(1)} %get-tuple-element.28), channel_id=1, source_target_pairs={{0,2},{1,3},{2,4},{3,5},{4,6},{5,7},{6,0},{7,1},{8,10},{9,11},{10,... | collective-permute-start | bytes 589832 | tf_op jit(solution)/shard_map/ppermute | solution.py:20
  79.1 8.3 %collective-permute-start.18 = (f32[96,512]{1,0:T(8,128)S(1)}, f32[96,512]{1,0:T(8,128)S(1)}, u32[]{:S(2)}, u32[]{:S(2)}) collective-permute-start(f32[96,512]{1,0:T(8,128)S(1)} %get-tuple-element.32), channel_id=1, source_target_pairs={{0,2},{1,3},{2,4},{3,5},{4,6},{5,7},{6,0},{7,1},{8,10},{9,11},{10,... | collective-permute-start | bytes 589832 | tf_op jit(solution)/shard_map/ppermute | solution.py:20
  79.2 8.2 %collective-permute-start.20 = (f32[96,512]{1,0:T(8,128)S(1)}, f32[96,512]{1,0:T(8,128)S(1)}, u32[]{:S(2)}, u32[]{:S(2)}) collective-permute-start(f32[96,512]{1,0:T(8,128)S(1)} %get-tuple-element.33), channel_id=1, source_target_pairs={{0,6},{1,7},{2,0},{3,1},{4,2},{5,3},{6,4},{7,5},{8,14},{9,15},{10,... | collective-permute-start | bytes 589832 | tf_op jit(solution)/shard_map/ppermute | solution.py:20
  84.1 10.1 %collective-permute-start.14 = (f32[192,512]{1,0:T(8,128)}, f32[192,512]{1,0:T(8,128)}, u32[]{:S(2)}, u32[]{:S(2)}) collective-permute-start(f32[192,512]{1,0:T(8,128)} %get-tuple-element.26), channel_id=1, source_target_pairs={{0,2},{1,3},{2,4},{3,5},{4,6},{5,7},{6,0},{7,1},{8,10},{9,11},{10,... | collective-permute-start | bytes 1179656 | tf_op jit(solution)/shard_map/ppermute | solution.py:20
  84.6 9.6 %collective-permute-start.16 = (f32[192,512]{1,0:T(8,128)}, f32[192,512]{1,0:T(8,128)}, u32[]{:S(2)}, u32[]{:S(2)}) collective-permute-start(f32[192,512]{1,0:T(8,128)} %get-tuple-element.27), channel_id=1, source_target_pairs={{0,6},{1,7},{2,0},{3,1},{4,2},{5,3},{6,4},{7,5},{8,14},{9,15},{10,... | collective-permute-start | bytes 1179656 | tf_op jit(solution)/shard_map/ppermute | solution.py:20
  88.4 14.3 %collective-permute-start.19 = (f32[192,512]{1,0:T(8,128)}, f32[192,512]{1,0:T(8,128)}, u32[]{:S(2)}, u32[]{:S(2)}) collective-permute-start(f32[192,512]{1,0:T(8,128)} %get-tuple-element.30), channel_id=1, source_target_pairs={{0,2},{1,3},{2,4},{3,5},{4,6},{5,7},{6,0},{7,1},{8,10},{9,11},{10,... | collective-permute-start | bytes 1179656 | tf_op jit(solution)/shard_map/ppermute | solution.py:20
  88.8 14.8 %collective-permute-start.21 = (f32[192,512]{1,0:T(8,128)}, f32[192,512]{1,0:T(8,128)}, u32[]{:S(2)}, u32[]{:S(2)}) collective-permute-start(f32[192,512]{1,0:T(8,128)} %get-tuple-element.31), channel_id=1, source_target_pairs={{0,6},{1,7},{2,0},{3,1},{4,2},{5,3},{6,4},{7,5},{8,14},{9,15},{10,... | collective-permute-start | bytes 1179656 | tf_op jit(solution)/shard_map/ppermute | solution.py:20
  91.0 15.9 %collective-permute-start.22 = (bf16[768,256]{1,0:T(8,128)(2,1)S(1)}, bf16[768,256]{1,0:T(8,128)(2,1)}, u32[]{:S(2)}, u32[]{:S(2)}) collective-permute-start(bf16[768,256]{1,0:T(8,128)(2,1)S(1)} %pad_maximum_fusion.3), channel_id=1, source_target_pairs={{0,16},{8,24},{16,0},{24,8},{1,17},{9,25},{17,1},{25,9},{2,18},{10... | collective-permute-start | bytes 1179656 | tf_op jit(solution)/shard_map/ppermute | solution.py:20
  94.2 12.8 %collective-permute-start.23 = (bf16[768,256]{1,0:T(8,128)(2,1)S(1)}, bf16[768,256]{1,0:T(8,128)(2,1)}, u32[]{:S(2)}, u32[]{:S(2)}) collective-permute-start(bf16[768,256]{1,0:T(8,128)(2,1)S(1)} %pad_maximum_fusion.3), channel_id=1, source_target_pairs={{0,24},{8,0},{16,8},{24,16},{1,25},{9,1},{17,9},{25,17},{2,26},{10... | collective-permute-start | bytes 1179656 | tf_op jit(solution)/shard_map/ppermute | solution.py:20
  94.2 16.0 %collective-permute-start.24 = (bf16[768,256]{1,0:T(8,128)(2,1)S(1)}, bf16[768,256]{1,0:T(8,128)(2,1)S(1)}, u32[]{:S(2)}, u32[]{:S(2)}) collective-permute-start(bf16[768,256]{1,0:T(8,128)(2,1)S(1)} %pad_maximum_fusion.3), channel_id=1, source_target_pairs={{0,8},{8,16},{16,24},{24,0},{1,9},{9,17},{17,25},{25,1},{2,10},{10... | collective-permute-start | bytes 1179656 | tf_op jit(solution)/shard_map/ppermute | solution.py:20
  102.6 12.1 %collective-permute-start.25 = (bf16[192,512]{1,0:T(8,128)(2,1)}, bf16[192,512]{1,0:T(8,128)(2,1)}, u32[]{:S(2)}, u32[]{:S(2)}) collective-permute-start(bf16[192,512]{1,0:T(8,128)(2,1)} %fusion.16), channel_id=1, source_target_pairs={{0,4},{1,5},{2,6},{3,7},{4,0},{5,1},{6,2},{7,3},{8,12},{9,13},{10,... | collective-permute-start | bytes 589832 | tf_op jit(solution)/shard_map/ppermute | solution.py:20
  103.6 11.9 %collective-permute-start.26 = (bf16[192,512]{1,0:T(8,128)(2,1)}, bf16[192,512]{1,0:T(8,128)(2,1)}, u32[]{:S(2)}, u32[]{:S(2)}) collective-permute-start(bf16[192,512]{1,0:T(8,128)(2,1)} %fusion.16), channel_id=1, source_target_pairs={{0,6},{1,7},{2,0},{3,1},{4,2},{5,3},{6,4},{7,5},{8,14},{9,15},{10,... | collective-permute-start | bytes 589832 | tf_op jit(solution)/shard_map/ppermute | solution.py:20
  106.9 8.7 %collective-permute-start.27 = (bf16[192,512]{1,0:T(8,128)(2,1)}, bf16[192,512]{1,0:T(8,128)(2,1)S(1)}, u32[]{:S(2)}, u32[]{:S(2)}) collective-permute-start(bf16[192,512]{1,0:T(8,128)(2,1)} %fusion.16), channel_id=1, source_target_pairs={{0,2},{1,3},{2,4},{3,5},{4,6},{5,7},{6,0},{7,1},{8,10},{9,11},{10,... | collective-permute-start | bytes 589832 | tf_op jit(solution)/shard_map/ppermute | solution.py:20
  106.9 15.0 %collective-permute-start.29 = (bf16[192,512]{1,0:T(8,128)(2,1)}, bf16[192,512]{1,0:T(8,128)(2,1)S(1)}, u32[]{:S(2)}, u32[]{:S(2)}) collective-permute-start(bf16[192,512]{1,0:T(8,128)(2,1)} %fusion.14), channel_id=1, source_target_pairs={{0,4},{1,5},{2,6},{3,7},{4,0},{5,1},{6,2},{7,3},{8,12},{9,13},{10,... | collective-permute-start | bytes 589832 | tf_op jit(solution)/shard_map/ppermute | solution.py:20
  110.2 11.8 %collective-permute-start.30 = (bf16[192,512]{1,0:T(8,128)(2,1)}, bf16[192,512]{1,0:T(8,128)(2,1)S(1)}, u32[]{:S(2)}, u32[]{:S(2)}) collective-permute-start(bf16[192,512]{1,0:T(8,128)(2,1)} %fusion.14), channel_id=1, source_target_pairs={{0,6},{1,7},{2,0},{3,1},{4,2},{5,3},{6,4},{7,5},{8,14},{9,15},{10,... | collective-permute-start | bytes 589832 | tf_op jit(solution)/shard_map/ppermute | solution.py:20
  114.7 9.0 %collective-permute-start.31 = (bf16[192,512]{1,0:T(8,128)(2,1)}, bf16[192,512]{1,0:T(8,128)(2,1)S(1)}, u32[]{:S(2)}, u32[]{:S(2)}) collective-permute-start(bf16[192,512]{1,0:T(8,128)(2,1)} %fusion.14), channel_id=1, source_target_pairs={{0,2},{1,3},{2,4},{3,5},{4,6},{5,7},{6,0},{7,1},{8,10},{9,11},{10,... | collective-permute-start | bytes 589832 | tf_op jit(solution)/shard_map/ppermute | solution.py:20
  117.3 11.2 %collective-permute-start.28 = (f32[512,512]{1,0:T(8,128)S(1)}, f32[512,512]{1,0:T(8,128)S(1)}, u32[]{:S(2)}, u32[]{:S(2)}) collective-permute-start(f32[512,512]{1,0:T(8,128)S(1)} %fusion.37), channel_id=1, source_target_pairs={{0,1},{1,0},{2,3},{3,2},{4,5},{5,4},{6,7},{7,6},{8,9},{9,8},{10,11... | collective-permute-start | bytes 3145736 | tf_op jit(solution)/shard_map/ppermute | solution.py:25
  134.6 33.6 %all-to-all-start.1 = ((bf16[8,64,1024]{2,1,0:T(8,128)(2,1)}), bf16[8,64,1024]{2,1,0:T(8,128)(2,1)S(1)}, u32[]{:S(2)}, u32[]{:S(2)}) async-start(bf16[8,64,1024]{2,1,0:T(8,128)(2,1)} %fusion.4), calls=%async_computation.1 | async-start | bytes 2097152 | tf_op jit(solution)/shard_map/all_to_all | solution.py:195
  (10 other events, 31.6 us)
